TPU v7x, 256 devices: a whole 4x4x8 slice. The times are simulated.
256 devices in a mesh: blk: 4 (over z_lo), sample: 64 (over y, x, z_hi, core).
Axes of the slice: x: 4, y: 4, z: 8 (z_hi: 2, z_lo: 4; z = z_hi * 4 + z_lo), core: 2. Of those that a mesh axis runs over, the one named last changes fastest.
Arguments:
- labels: bfloat16 [64, 4096, 512], P('sample', 'blk'), may hold values from -6 to 6
- basis: bfloat16 [64, 4096, 1024], P('sample', 'blk'), may hold values from -0.01171875 to 0.01171875
- gains: float32 [1024], replicated, may hold values from 2 to 32
- tiles: bfloat16 [64, 16, 4, 256, 256], P('sample', 'blk'), may hold values from 0 to 0.0029296875
- tile_cols: int32 [64, 16, 4], P('sample', 'blk'), may hold values from 0 to 15
- tile_valid: int32 [64, 16, 4], P('sample', 'blk'), may hold values 0 or 1
Outputs:
- solution: float32 [64, 4096, 512], P('sample', 'blk')
- residual: float32 [64, 4096, 512], P('sample', 'blk')
All inputs are finite; a program needn't handle non-finite values. No bound on the sum of `tile_valid` on one device may be relied on, other than what follows from the above.
Results may differ from a plain program's by a relative error of at most 0.0022.
Values may be sent and summed in bfloat16 or wider, within the bound.
No kernel may reach another device: no remote copies, remote signals or barrier semaphores. Data moves between devices by JAX's collectives and lax.ppermute only.
A program may use at most 64 MiB of HBM per device.

v0:
```python
import jax
import jax.numpy as jnp
from jax import lax
from jax.sharding import PartitionSpec as P


def on_device(labels, basis, gains, tiles, tile_cols, tile_valid):
    rows_dev = labels.shape[1]
    classes = labels.shape[2]
    rank_size = basis.shape[2]
    row_blocks = tiles.shape[1]
    slot_count = tiles.shape[2]
    tile_size = tiles.shape[3]
    group_size = lax.axis_size("blk")
    col_blocks = row_blocks * group_size
    slots_all = row_blocks * slot_count
    tiles_flat = tiles.reshape(slots_all, tile_size, tile_size)
    cols_flat = tile_cols.reshape(slots_all)
    valid_flat = tile_valid.reshape(slots_all).astype(jnp.float32)
    basis_rows = basis[0]
    row_part = jnp.sum(tiles_flat, axis=2, dtype=jnp.float32)
    row_total = jnp.sum(
        (row_part * valid_flat[:, None]).reshape(row_blocks, slot_count, tile_size), axis=1
    ).reshape(rows_dev)
    col_part = jnp.sum(tiles_flat, axis=1, dtype=jnp.float32)
    onehot = (cols_flat[:, None] == jnp.arange(col_blocks, dtype=jnp.int32)[None, :]).astype(
        jnp.float32
    ) * valid_flat[:, None]
    spread_cols = jnp.dot(onehot.T, col_part, precision=lax.Precision.HIGHEST)
    own_cols = lax.psum_scatter(spread_cols, "blk", scatter_dimension=0, tiled=True)
    degree = 0.5 * (row_total + own_cols.reshape(rows_dev))

    def col_dot(first, second):
        return lax.psum(jnp.sum(first * second, axis=0), ("blk", "sample"))

    residual = labels[0].astype(jnp.float32)
    rounded = residual.astype(jnp.bfloat16)
    share_rows = rank_size // lax.axis_size(("blk", "sample"))
    share = lax.psum_scatter(
        lax.dot_general(
            basis_rows, rounded, (((0,), (0,)), ((), ())), preferred_element_type=jnp.float32
        ),
        ("blk", "sample"),
        scatter_dimension=0,
        tiled=True,
    )
    offset = lax.axis_index(("blk", "sample")) * share_rows
    local_gain = lax.dynamic_slice_in_dim(gains, offset, share_rows)
    coeffs = (local_gain[:, None] * share).astype(jnp.bfloat16)
    all_coeffs = lax.all_gather(coeffs, ("blk", "sample"), axis=0, tiled=True)
    result = jnp.dot(basis_rows, all_coeffs, preferred_element_type=jnp.float32)
    search = residual + result
    norm_now = col_dot(residual, search)
    panel = search.astype(jnp.bfloat16)
    piece = lax.all_gather(panel, "blk", axis=0, tiled=True)
    count = piece.shape[0] // tile_size
    blocks = piece.reshape(count, tile_size, classes)
    first = jnp.int32(0) // tile_size
    hits = (cols_flat[:, None] == jnp.arange(count, dtype=jnp.int32)[None, :]).astype(jnp.bfloat16)
    chosen = jnp.einsum("sj,jik->sik", hits, blocks, preferred_element_type=jnp.float32).astype(
        jnp.bfloat16
    )
    product = jnp.einsum("sij,sjk->sik", tiles_flat, chosen, preferred_element_type=jnp.float32)
    weighted = jnp.sum(
        (product * valid_flat[:, None, None]).reshape(row_blocks, slot_count, tile_size, classes),
        axis=1,
    ).reshape(rows_dev, classes)
    image = search + 0.5 * (degree[:, None] * search - weighted)
    step_size = norm_now / col_dot(search, image)
    solution = step_size * search
    residual = residual - step_size * image
    return (solution[None], residual[None])


def solution(mesh):
    return jax.shard_map(
        on_device,
        mesh=mesh,
        in_specs=(
            P("sample", "blk", None),
            P("sample", "blk", None),
            P(),
            P("sample", "blk", None, None, None),
            P("sample", "blk", None),
            P("sample", "blk", None),
        ),
        out_specs=(P("sample", "blk", None), P("sample", "blk", None)),
        check_vma=False,
    )
```

profile of v0, /device:TPU:1, one launch (start us, length us, event | category | flops | bytes accessed | tf_op | source)
XLA Modules:
  0.0 869.3 jit_solution(6628905587682090301)
XLA Ops:
  7.2 1.5 copy-done
  8.8 3.8 fusion.8
  12.7 0.8 dynamic_slice.3
  13.4 264.0 %all-reduce.5.cloned.1.call-done = f32[1024,512]{1,0:T(8,128)} async-done(((f32[1024,512]{1,0:T(8,128)}), f32[1024,512]{1,0:T(8,128)}) %all-reduce.5.cloned.1.call-update) | async-done | bytes 2097168
  277.4 1.4 fusion.18
  278.9 1.5 copy.15
  280.3 378.4 %all-gather.6.cloned.1.call-done = bf16[256,4,512]{2,1,0:T(4,128)(2,1)} async-done(((bf16[1,4,512]{2,1,0:T(4,128)(2,1)}), bf16[256,4,512]{2,1,0:T(4,128)(2,1)}) %all-gather.6.cloned.1.call-update) | async-done | bytes 1048592 | tf_op jit(solution)/shard_map/all_gather | solution.py:50
  658.8 2.1 reshape.63
  660.9 4.2 fusion.26
  665.3 2.4 convert_reduce_fusion
  667.8 0.6 dynamic-slice.1
  669.0 0.3 fusion.14
  669.3 14.2 %all-reduce.1 = f32[16,256]{1,0:T(8,128)S(1)} all-reduce(f32[16,256]{1,0:T(8,128)S(1)} %fusion.14), channel_id=3, replica_groups=mesh['blk'=4,'sample'=64] {'blk'}, use_global_device_ids=true, to_apply=%region_6.0.clone | all-reduce | flops 4096 | bytes 32768
  683.6 63.0 %all-gather.4.cloned.1.call-done = bf16[4096,512]{0,1:T(8,128)(2,1)} async-done(((bf16[1024,512]{0,1:T(8,128)(2,1)}), bf16[4096,512]{0,1:T(8,128)(2,1)}) %all-gather.4.cloned.1.call-update) | async-done | bytes 4194320 | tf_op jit(solution)/shard_map/all_gather | solution.py:55
  746.6 5.6 copy.23
  752.2 8.6 copy.16
  760.8 3.6 convolution_convert_fusion
  764.5 5.7 bitcast_reduce_fusion
  770.5 2.1 copy-done.2
  772.6 0.7 multiply_reduce_fusion
  773.3 78.9 %all-reduce.2 = (f32[512]{0:T(512)S(1)}, f32[512]{0:T(512)S(1)}) all-reduce(f32[512]{0:T(512)S(1)} %get-tuple-element.9, f32[512]{0:T(512)S(1)} %get-tuple-element.8), channel_id=1, replica_groups=mesh['blk'=4,'sample'=64] {'blk','sample'}, use_global_device_ids=true, to_apply=%region_2.0 | all-reduce | flops 1024 | bytes 8192 | tf_op jit(solution)/shard_map/psum | solution.py:34
  852.2 4.8 fusion.5
  857.0 2.9 copy.19
  859.9 2.9 copy.20
  (27 shorter events, 0.7 us)
Async XLA Ops:
  7.2 1.6 copy-start
  7.2 270.2 %all-reduce.5.cloned.1.call-start = ((), (), s32[]{:S(2)}) async-start(), calls=%async_computation.2 | async-start | bytes 4194304
  12.6 646.2 %all-gather.6.cloned.1.call-start = ((), (), s32[]{:S(2)}) async-start(), calls=%async_computation.1 | async-start | bytes 1052672 | tf_op jit(solution)/shard_map/all_gather | solution.py:50
  278.8 467.8 %all-gather.4.cloned.1.call-start = ((), (), s32[]{:S(2)}) async-start(), calls=%async_computation | async-start | bytes 5242880 | tf_op jit(solution)/shard_map/all_gather | solution.py:55
  660.9 4.2 copy-start.5
  660.9 4.3 copy-start.4
  665.1 2.7 copy-start.6
  760.8 3.6 copy-start.3
  770.2 2.4 copy-start.2
  770.5 2.8 copy-start.1
Sparse Core Ops, SparseCore 0:
  14.0 263.3 all-reduce.4
  279.8 378.9 all-gather.5
  665.3 81.3 all-gather.3
where the time goes:
time: 870 us; the launch traced here: 869 us
  waiting for transfers between devices  705 us (81%)
  blocking collectives  93.1 us (11%)
  local copies, waits for them, and re-layouts  29 us (3%)
  matrix products  17.7 us (2%)
  between operations  14.5 us (2%)
  other arithmetic  9.49 us (1%)
    all_gather x1, waiting for transfers between devices, on_device(): all_coeffs = lax.all_gather(coeffs, ('blk', 'sample'), axis=0, tiled=True)  378 us
    unnamed x4, waiting for transfers between devices  264 us
    psum x1, blocking collectives, col_dot(): return lax.psum(jnp.sum(first * second, axis=0), ('blk', 'sample'))  78.9 us
    all_gather x1, waiting for transfers between devices, on_device(): piece = lax.all_gather(panel, 'blk', axis=0, tiled=True)  63 us
    unnamed x21, local copies, waits for them, and re-layouts  19.2 us
  transfers between devices with their start and end apart: 3, of which 3 were waited for; matrix products, arithmetic and copies ran while one was open for 1% of the time, Pallas kernels for 0%

commit v1 on v0

v1 whole, which is shorter than its diff:
```python
import jax
import jax.numpy as jnp
from jax import lax
from jax.experimental import pallas as pl
from jax.experimental.pallas import tpu as pltpu
from jax.sharding import Mesh, PartitionSpec as P

F32 = jnp.float32
BF16 = jnp.bfloat16
FINE = ("blk", "y", "x", "zh", "core")
SAMPLE = ("y", "x", "zh", "core")
VMEM_LIMIT = 48 * 1024 * 1024


def shift(value, axis, by):
    size = lax.axis_size(axis)
    return lax.ppermute(value, axis, [(i, (i + by) % size) for i in range(size)])


def along_line(value, by, skip):
    size = lax.axis_size("blk")
    if by > 0:
        pairs = [(i, i + 1) for i in range(skip, size - 1)]
    else:
        pairs = [(i, i - 1) for i in range(1, size - skip)]
    return lax.ppermute(value, "blk", pairs)


def reduce_scatter(value, axis):
    size = lax.axis_size(axis)
    me = lax.axis_index(axis)
    rows = value.shape[0] // size
    parts = [
        lax.dynamic_slice_in_dim(value, ((me + k) % size) * rows, rows) for k in range(size)
    ]
    got = [shift(parts[k], axis, k) for k in range(1, size)]
    total = parts[0]
    for part in got:
        total = total + part
    return total


def all_sum(value, axis):
    total = value
    for part in [shift(value, axis, k) for k in range(1, lax.axis_size(axis))]:
        total = total + part
    return total


def degree_parts_kernel(cols, valid, tiles, rows_out, cols_out):
    step = pl.program_id(0)
    slots = tiles.shape[0]

    @pl.when(step == 0)
    def _():
        cols_out[...] = jnp.zeros_like(cols_out)

    total = jnp.zeros(tiles.shape[1:], F32)
    for t in range(slots):
        at = step * slots + t
        tile = tiles[t].astype(F32) * valid[at].astype(F32)
        total = total + tile
        cols_out[pl.ds(cols[at], 1), :] += jnp.sum(tile, axis=0, keepdims=True)
    rows_out[...] = jnp.sum(total, axis=1, keepdims=True)


def degree_parts(tiles, cols, valid, col_blocks, slots):
    count, size, _ = tiles.shape
    steps = count // slots
    return pl.pallas_call(
        degree_parts_kernel,
        grid_spec=pltpu.PrefetchScalarGridSpec(
            num_scalar_prefetch=2,
            grid=(steps,),
            in_specs=[pl.BlockSpec((slots, size, size), lambda i, c, v: (i, 0, 0))],
            out_specs=[
                pl.BlockSpec((size, 1), lambda i, c, v: (i, 0)),
                pl.BlockSpec((col_blocks, size), lambda i, c, v: (0, 0)),
            ],
        ),
        out_shape=[
            jax.ShapeDtypeStruct((steps * size, 1), F32),
            jax.ShapeDtypeStruct((col_blocks, size), F32),
        ],
        cost_estimate=pl.CostEstimate(
            flops=4 * tiles.size, bytes_accessed=2 * tiles.size, transcendentals=0
        ),
        name="degree_parts",
    )(cols, valid, tiles)


def spread_kernel(place, labels, basis, mine, theirs, search, rounded, dots, coeffs):
    step = pl.program_id(0)
    rows = mine.shape[1]
    parts = mine.shape[0]

    @pl.when(step == 0)
    def _():
        dots[...] = jnp.zeros_like(dots)
        for k in range(parts):
            at = place[0] * parts + lax.rem(place[1] + parts - k, parts)
            coeffs[pl.ds(pl.multiple_of(at * rows, rows), rows), :] = mine[k]
            at = (1 - place[0]) * parts + lax.rem(place[1] + parts - k, parts)
            coeffs[pl.ds(pl.multiple_of(at * rows, rows), rows), :] = theirs[k]

    residual = labels[...].astype(F32)
    value = residual + jnp.dot(basis[...], coeffs[...], preferred_element_type=F32)
    search[...] = value
    rounded[...] = value.astype(BF16)
    dots[...] += jnp.sum(residual * value, axis=0, keepdims=True)


def spread(place, labels, basis, mine, theirs):
    rows, classes = labels.shape
    rank = basis.shape[1]
    steps = 4
    part = rows // steps
    return pl.pallas_call(
        spread_kernel,
        grid_spec=pltpu.PrefetchScalarGridSpec(
            num_scalar_prefetch=1,
            grid=(steps,),
            in_specs=[
                pl.BlockSpec((part, classes), lambda i, p: (i, 0)),
                pl.BlockSpec((part, rank), lambda i, p: (i, 0)),
                pl.BlockSpec(mine.shape, lambda i, p: (0, 0, 0)),
                pl.BlockSpec(theirs.shape, lambda i, p: (0, 0, 0)),
            ],
            out_specs=[
                pl.BlockSpec((part, classes), lambda i, p: (i, 0)),
                pl.BlockSpec((part, classes), lambda i, p: (i, 0)),
                pl.BlockSpec((1, classes), lambda i, p: (0, 0)),
            ],
            scratch_shapes=[pltpu.VMEM((rank, classes), BF16)],
        ),
        out_shape=[
            jax.ShapeDtypeStruct((rows, classes), F32),
            jax.ShapeDtypeStruct((rows, classes), BF16),
            jax.ShapeDtypeStruct((1, classes), F32),
        ],
        compiler_params=pltpu.CompilerParams(vmem_limit_bytes=VMEM_LIMIT),
        name="spread",
    )(place, labels, basis, mine, theirs)


def apply_kernel(
    cols, valid, place, tiles, degree, search, own, l1, l2, l3, r1, r2, r3, image, dots, panel
):
    step = pl.program_id(0)
    slots, size, _ = tiles.shape
    rows = own.shape[0]
    me = place[2]
    last = panel.shape[0] // rows - 1

    @pl.when(step == 0)
    def _():
        dots[...] = jnp.zeros_like(dots)
        panel[pl.ds(pl.multiple_of(me * rows, rows), rows), :] = own[...]
        for k, (left, right) in enumerate(((l1, r1), (l2, r2), (l3, r3)), 1):

            @pl.when(me >= k)
            def _(left=left, k=k):
                panel[pl.ds(pl.multiple_of((me - k) * rows, rows), rows), :] = left[...]

            @pl.when(me + k <= last)
            def _(right=right, k=k):
                panel[pl.ds(pl.multiple_of((me + k) * rows, rows), rows), :] = right[...]

    total = jnp.zeros(search.shape, F32)
    for t in range(slots):
        at = step * slots + t
        block = panel[pl.ds(pl.multiple_of(cols[at] * size, size), size), :]
        product = jnp.dot(tiles[t], block, preferred_element_type=F32)
        total = total + product * valid[at].astype(F32)
    value = search[...]
    result = value + 0.5 * (degree[...] * value - total)
    image[...] = result
    dots[...] += jnp.sum(value * result, axis=0, keepdims=True)


def apply(cols, valid, place, tiles, degree, search, own, received, slots):
    rows, classes = search.shape
    count, size, _ = tiles.shape
    steps = count // slots
    whole = pl.BlockSpec((rows, classes), lambda i, c, v, p: (0, 0))
    return pl.pallas_call(
        apply_kernel,
        grid_spec=pltpu.PrefetchScalarGridSpec(
            num_scalar_prefetch=3,
            grid=(steps,),
            in_specs=[
                pl.BlockSpec((slots, size, size), lambda i, c, v, p: (i, 0, 0)),
                pl.BlockSpec((size, 1), lambda i, c, v, p: (i, 0)),
                pl.BlockSpec((size, classes), lambda i, c, v, p: (i, 0)),
            ]
            + [whole] * 7,
            out_specs=[
                pl.BlockSpec((size, classes), lambda i, c, v, p: (i, 0)),
                pl.BlockSpec((1, classes), lambda i, c, v, p: (0, 0)),
            ],
            scratch_shapes=[pltpu.VMEM((4 * rows, classes), BF16)],
        ),
        out_shape=[
            jax.ShapeDtypeStruct((rows, classes), F32),
            jax.ShapeDtypeStruct((1, classes), F32),
        ],
        compiler_params=pltpu.CompilerParams(vmem_limit_bytes=VMEM_LIMIT),
        name="apply",
    )(cols, valid, place, tiles, degree, search, own, *received)


def step_kernel(sums, labels, search, image, solution_out, residual_out):
    size = sums[0:1, :] / sums[1:2, :]
    solution_out[...] = size * search[...]
    residual_out[...] = labels[...].astype(F32) - size * image[...]


def take_step(sums, labels, search, image):
    rows, classes = search.shape
    steps = 4
    part = rows // steps
    block = pl.BlockSpec((part, classes), lambda i: (i, 0))
    return pl.pallas_call(
        step_kernel,
        grid=(steps,),
        in_specs=[pl.BlockSpec(sums.shape, lambda i: (0, 0)), block, block, block],
        out_specs=[block, block],
        out_shape=[jax.ShapeDtypeStruct((rows, classes), F32)] * 2,
        compiler_params=pltpu.CompilerParams(vmem_limit_bytes=VMEM_LIMIT),
        name="take_step",
    )(sums, labels, search, image)


def on_device(labels, basis, gains, tiles, tile_cols, tile_valid):
    labels, basis, tiles = labels[0], basis[0], tiles[0]
    rows_dev, classes = labels.shape
    rank = basis.shape[1]
    row_blocks, slots, tile_size = tiles.shape[:3]
    group = lax.axis_size("blk")
    tiles = tiles.reshape(row_blocks * slots, tile_size, tile_size)
    cols = tile_cols.reshape(-1)
    valid = tile_valid.reshape(-1)
    blk, y, x, core = (lax.axis_index(a) for a in ("blk", "y", "x", "core"))
    place = jnp.stack([core, x, blk]).astype(jnp.int32)

    row_total, col_parts = degree_parts(tiles, cols, valid, row_blocks * group, slots)
    col_parts = col_parts.reshape(group * rows_dev // classes, classes)
    extra = rows_dev // classes

    partial = lax.dot_general(
        basis, labels, (((0,), (0,)), ((), ())), preferred_element_type=F32
    )
    share = partial
    for axis in ("core", "x", "y"):
        share = reduce_scatter(share, axis)
    share_rows = share.shape[0]

    def with_cols(k):
        part = lax.dynamic_slice_in_dim(col_parts, ((blk + k) % group) * extra, extra)
        return jnp.concatenate([share, part], axis=0)

    joined = with_cols(0)
    for part in [shift(with_cols(k), "blk", k) for k in range(1, group)]:
        joined = joined + part
    share = joined[:share_rows]
    share = share + shift(share, "zh", 1)
    degree = 0.5 * (row_total + joined[share_rows:].reshape(rows_dev, 1))

    offset = (core * lax.axis_size("x") + x) * (share_rows * lax.axis_size("y")) + y * share_rows
    local_gain = lax.dynamic_slice_in_dim(gains, offset, share_rows)
    coeffs = (local_gain[:, None] * share).astype(BF16)
    size_y = lax.axis_size("y")
    over_y = jnp.zeros((size_y * share_rows, classes), BF16)
    for k, part in enumerate([coeffs] + [shift(coeffs, "y", k) for k in range(1, size_y)]):
        over_y = lax.dynamic_update_slice_in_dim(
            over_y, part, ((y + size_y - k) % size_y) * share_rows, 0
        )
    size_x = lax.axis_size("x")
    mine = jnp.stack([over_y] + [shift(over_y, "x", k) for k in range(1, size_x)])
    theirs = shift(mine, "core", 1)

    search, rounded, dot_rz = spread(place, labels, basis, mine, theirs)
    l1, r1 = along_line(rounded, 1, 0), along_line(rounded, -1, 0)
    l2, r2 = along_line(l1, 1, 1), along_line(r1, -1, 1)
    l3, r3 = along_line(l2, 1, 2), along_line(r2, -1, 2)
    image, dot_image = apply(
        cols, valid, place, tiles, degree, search, rounded, (l1, l2, l3, r1, r2, r3), slots
    )
    sums = jnp.concatenate([dot_rz, dot_image], axis=0)
    for axis in ("core", "x", "y", "blk", "zh"):
        sums = all_sum(sums, axis)
    solution_out, residual_out = take_step(sums, labels, search, image)
    return solution_out[None], residual_out[None]


def solution(mesh):
    blk, sample = mesh.devices.shape
    fine = Mesh(mesh.devices.reshape(blk, 4, 4, 2, sample // 32), FINE)
    return jax.shard_map(
        on_device,
        mesh=fine,
        in_specs=(
            P(SAMPLE, "blk", None),
            P(SAMPLE, "blk", None),
            P(),
            P(SAMPLE, "blk", None, None, None),
            P(SAMPLE, "blk", None),
            P(SAMPLE, "blk", None),
        ),
        out_specs=(P(SAMPLE, "blk", None), P(SAMPLE, "blk", None)),
        check_vma=False,
    )
```

time: 870 us -> 205 us (0.24)
  waiting for transfers between devices: 705 us -> 101 us
  blocking collectives: 93.1 us -> 0 us
  starting transfers between devices: 0.12 us -> 63.4 us
  local copies, waits for them, and re-layouts: 29 us -> 9.13 us
  Pallas kernels: 0 us -> 18.4 us
  between operations: 14.5 us -> 0.88 us
  matrix products: 17.7 us -> 4.46 us
    all_gather x2 -> x0, waiting for transfers between devices: 441 us -> none  [the longest x1 378 us: on_device(): all_coeffs = lax.all_gather(coeffs, ('blk', 'sample'), axis=0, tiled=True)]
    unnamed x4 -> x0, waiting for transfers between devices: 264 us -> none
    ppermute x0 -> x35, waiting for transfers between devices: none -> 101 us  [the longest x6 61.8 us: along_line(): return lax.ppermute(value, 'blk', pairs)]
    psum x1 -> x0, blocking collectives: 78.9 us -> none  [col_dot(): return lax.psum(jnp.sum(first * second, axis=0), ('blk', 'sample'))]
    ppermute x0 -> x35, starting transfers between devices: none -> 63.4 us  [the longest x29 52 us: shift(): lax.ppermute(value, axis, [(i, (i + by) % size) for i in range(size)])]
    pallas_call x0 -> x4, Pallas kernels: none -> 18.4 us  [the longest x1 7.3 us: apply(): pl.pallas_call(apply_kernel, grid_spec=pltpu.PrefetchScalarGridSpec(num_s...]
    unnamed x21 -> x23, local copies, waits for them, and re-layouts: 19.2 us -> 4.95 us
    unnamed x1 -> x0, blocking collectives: 14.2 us -> none
  transfers between devices with their start and end apart: 3 -> 35, of which waited for: 3 -> 27; matrix products, arithmetic and copies ran while one was open for 1% -> 3% of each run, Pallas kernels for 0% -> 2%
where the time goes in v1:
time: 205 us; the launch traced here: 201 us
  waiting for transfers between devices  101 us (49%)
  starting transfers between devices  63.4 us (31%)
  Pallas kernels  18.4 us (9%)
  local copies, waits for them, and re-layouts  9.13 us (4%)
  matrix products  4.46 us (2%)
  other arithmetic  4.14 us (2%)
    ppermute x6, waiting for transfers between devices, along_line(): return lax.ppermute(value, 'blk', pairs)  61.8 us
    ppermute x29, starting transfers between devices, shift(): lax.ppermute(value, axis, [(i, (i + by) % size) for i in range(size)])  52 us
    ppermute x29, waiting for transfers between devices, shift(): lax.ppermute(value, axis, [(i, (i + by) % size) for i in range(size)])  39 us
    ppermute x6, starting transfers between devices, along_line(): return lax.ppermute(value, 'blk', pairs)  11.3 us
    pallas_call x1, Pallas kernels, apply(): pl.pallas_call(apply_kernel, grid_spec=pltpu.PrefetchScalarGridSpec(num_s...  7.3 us
    unnamed x23, local copies, waits for them, and re-layouts  4.95 us
    pallas_call x1, Pallas kernels, degree_parts(): pl.pallas_call(degree_parts_kernel, grid_spec=pltpu.PrefetchScalarGridSpe...  4.52 us
    dot_general x1, matrix products, on_device(): lax.dot_general(basis, labels, (((0,), (0,)), ((), ())), preferred_elemen...  4.46 us
  transfers between devices with their start and end apart: 35, of which 27 were waited for; matrix products, arithmetic and copies ran while one was open for 3% of the time, Pallas kernels for 2%

profile of v1, /device:TPU:1, one launch (start us, length us, event | category | flops | bytes accessed | tf_op | source)
XLA Modules:
  0.0 201.2 jit_solution(13737542070985017429)
XLA Ops:
  0.6 4.5 %fusion.4 = f32[1024,512]{1,0:T(8,128)} fusion(bf16[1,1024,1024]{2,1,0:T(8,128)(2,1)} %param.7, bf16[1,1024,512]{2,1,0:T(8,128)(2,1)} %param.6), kind=kOutput, calls=%fused_computation.35 | convolution fusion | flops 1073741824 | bytes 5242880 | tf_op jit(solution)/shard_map/dot_general | solution.py:250
  6.4 3.3 %collective-permute-start = (f32[512,512]{1,0:T(8,128)S(1)}, f32[512,512]{1,0:T(8,128)S(1)}, u32[]{:S(2)}, u32[]{:S(2)}) collective-permute-start(f32[512,512]{1,0:T(8,128)S(1)} %constant_dynamic-slice_fusion.10), channel_id=1, source_target_pairs={{0,1},{1,0},{2,3},{3,2},{4,5},{5,4},{6,7},{7,6},{8,9},{9,8},{10,11... | collective-permute-start | bytes 3145736 | tf_op jit(solution)/shard_map/ppermute | solution.py:17
  9.7 2.3 %collective-permute-done = f32[512,512]{1,0:T(8,128)S(1)} collective-permute-done((f32[512,512]{1,0:T(8,128)S(1)}, f32[512,512]{1,0:T(8,128)S(1)}, u32[]{:S(2)}, u32[]{:S(2)}) %collective-permute-start) | collective-permute-done | bytes 1048608 | tf_op jit(solution)/shard_map/ppermute | solution.py:17
  13.6 2.7 %collective-permute-start.3 = (f32[128,512]{1,0:T(8,128)S(1)}, f32[128,512]{1,0:T(8,128)S(1)}, u32[]{:S(2)}, u32[]{:S(2)}) collective-permute-start(f32[128,512]{1,0:T(8,128)S(1)} %get-tuple-element.23), channel_id=1, source_target_pairs={{0,12},{4,0},{8,4},{12,8},{1,13},{5,1},{9,5},{13,9},{2,14},{6,2},{... | collective-permute-start | bytes 786440 | tf_op jit(solution)/shard_map/ppermute | solution.py:17
  17.6 4.5 %degree_parts.1 = (f32[1024,1]{1,0:T(8,128)}, f32[16,256]{1,0:T(8,128)}) custom-call(s32[16]{0:T(128)} %reshape.17.cols, s32[16]{0:T(128)} %reshape.18.valid, bf16[16,256,256]{2,1,0:T(8,128)(2,1)} %bitcast.26), custom_call_target="tpu_custom_call" | custom-call | flops 4194304 | bytes 2097152 | tf_op jit(solution)/shard_map/degree_parts/pallas_call | solution.py:70
  23.1 4.3 %collective-permute-done.2 = f32[128,512]{1,0:T(8,128)} collective-permute-done((f32[128,512]{1,0:T(8,128)S(1)}, f32[128,512]{1,0:T(8,128)}, u32[]{:S(2)}, u32[]{:S(2)}) %collective-permute-start.2) | collective-permute-done | bytes 262176 | tf_op jit(solution)/shard_map/ppermute | solution.py:17
  32.9 3.5 %collective-permute-done.5 = f32[32,512]{1,0:T(8,128)S(1)} collective-permute-done((f32[32,512]{1,0:T(8,128)S(1)}, f32[32,512]{1,0:T(8,128)S(1)}, u32[]{:S(2)}, u32[]{:S(2)}) %collective-permute-start.5) | collective-permute-done | bytes 65568 | tf_op jit(solution)/shard_map/ppermute | solution.py:17
  38.1 3.0 %collective-permute-start.8 = (f32[34,512]{1,0:T(8,128)S(1)}, f32[34,512]{1,0:T(8,128)S(1)}, u32[]{:S(2)}, u32[]{:S(2)}) collective-permute-start(f32[34,512]{1,0:T(8,128)S(1)} %get-tuple-element.29), channel_id=1, source_target_pairs={{0,128},{64,192},{128,0},{192,64},{1,129},{65,193},{129,1},{193,65... | collective-permute-start | bytes 208904 | tf_op jit(solution)/shard_map/ppermute | solution.py:17
  46.5 3.7 %collective-permute-start.10 = (f32[32,512]{1,0:T(8,128)S(1)}, f32[32,512]{1,0:T(8,128)S(1)}, u32[]{:S(2)}, u32[]{:S(2)}) collective-permute-start(f32[32,512]{1,0:T(8,128)S(1)} %slice.8), channel_id=1, source_target_pairs={{0,2},{2,0},{1,3},{3,1},{4,6},{6,4},{5,7},{7,5},{8,10},{10,8},{9,1... | collective-permute-start | bytes 196616 | tf_op jit(solution)/shard_map/ppermute | solution.py:17
  51.0 2.7 %collective-permute-done.10 = f32[32,512]{1,0:T(8,128)S(1)} collective-permute-done((f32[32,512]{1,0:T(8,128)S(1)}, f32[32,512]{1,0:T(8,128)S(1)}, u32[]{:S(2)}, u32[]{:S(2)}) %collective-permute-start.10) | collective-permute-done | bytes 65568 | tf_op jit(solution)/shard_map/ppermute | solution.py:17
  53.8 2.9 %collective-permute-start.12 = (bf16[32,512]{1,0:T(8,128)(2,1)S(1)}, bf16[32,512]{1,0:T(8,128)(2,1)S(1)}, u32[]{:S(2)}, u32[]{:S(2)}) collective-permute-start(bf16[32,512]{1,0:T(8,128)(2,1)S(1)} %get-tuple-element.21), channel_id=1, source_target_pairs={{0,32},{16,48},{32,0},{48,16},{1,33},{17,49},{33,1},{49,17},{2,34}... | collective-permute-start | bytes 98312 | tf_op jit(solution)/shard_map/ppermute | solution.py:17
  66.8 7.5 %collective-permute-start.17 = (bf16[4,128,512]{2,1,0:T(8,128)(2,1)S(1)}, bf16[4,128,512]{2,1,0:T(8,128)(2,1)S(1)}, u32[]{:S(2)}, u32[]{:S(2)}) collective-permute-start(bf16[4,128,512]{2,1,0:T(8,128)(2,1)S(1)} %pad_maximum_fusion.mine), channel_id=1, source_target_pairs={{0,1},{1,0},{2,3},{3,2},{4,5},{5,4},{6,7},{7,6},{8,9},{9,8},{10,11... | collective-permute-start | bytes 1572872 | tf_op jit(solution)/shard_map/ppermute | solution.py:17
  75.9 4.2 %spread.1 = (f32[1024,512]{1,0:T(8,128)S(1)}, bf16[1024,512]{1,0:T(8,128)(2,1)S(1)}, f32[1,512]{1,0:T(1,128)S(1)}) custom-call(s32[3]{0:T(128)S(1)} %pad_add_fusion.place, bf16[1024,512]{1,0:T(8,128)(2,1)S(1)} %bitcast.24, bf16[1024,1024]{1,0:T(8,128)(2,1)} %bitcast.28, bf16[4,128,512]{2,1,0:T(8,128)(2,1)S(1)} %pad_maximum_fusion.mine, ...), custom_call_target="tpu_custom_call" | custom-call | tf_op jit(solution)/shard_map/spread/pallas_call | solution.py:118
  82.8 4.1 %collective-permute-start.18 = (bf16[1024,512]{1,0:T(8,128)(2,1)S(1)}, bf16[1024,512]{1,0:T(8,128)(2,1)S(1)}, u32[]{:S(2)}, u32[]{:S(2)}) collective-permute-start(bf16[1024,512]{1,0:T(8,128)(2,1)S(1)} %get-tuple-element.15.own), channel_id=1, source_target_pairs={{0,64},{64,128},{128,192},{1,65},{65,129},{129,193},{2,66},{66,130... | collective-permute-start | bytes 3145736 | tf_op jit(solution)/shard_map/ppermute | solution.py:26
  86.9 20.9 %collective-permute-done.21.r1 = bf16[1024,512]{1,0:T(8,128)(2,1)S(1)} collective-permute-done((bf16[1024,512]{1,0:T(8,128)(2,1)S(1)}, bf16[1024,512]{1,0:T(8,128)(2,1)S(1)}, u32[]{:S(2)}, u32[]{:S(2)}) %collective-permute-start.21) | collective-permute-done | bytes 1048608 | tf_op jit(solution)/shard_map/ppermute | solution.py:26
  111.7 21.5 %collective-permute-done.22.r2 = bf16[1024,512]{1,0:T(8,128)(2,1)} collective-permute-done((bf16[1024,512]{1,0:T(8,128)(2,1)S(1)}, bf16[1024,512]{1,0:T(8,128)(2,1)}, u32[]{:S(2)}, u32[]{:S(2)}) %collective-permute-start.22) | collective-permute-done | bytes 1048608 | tf_op jit(solution)/shard_map/ppermute | solution.py:26
  138.6 19.4 %collective-permute-done.23.r3 = bf16[1024,512]{1,0:T(8,128)(2,1)} collective-permute-done((bf16[1024,512]{1,0:T(8,128)(2,1)}, bf16[1024,512]{1,0:T(8,128)(2,1)}, u32[]{:S(2)}, u32[]{:S(2)}) %collective-permute-start.23) | collective-permute-done | bytes 1048608 | tf_op jit(solution)/shard_map/ppermute | solution.py:26
  158.0 7.3 %apply.1 = (f32[1024,512]{1,0:T(8,128)}, f32[1,512]{1,0:T(1,128)S(1)}) custom-call(s32[16]{0:T(128)S(1)} %copy-done.6, s32[16]{0:T(128)S(1)} %copy-done.7, s32[3]{0:T(128)S(1)} %pad_add_fusion.place, bf16[16,256,256]{2,1,0:T(8,128)(2,1)} %bitcast.27, f32[1024,1]{1,0:T(8,128)S(1)} %fusion.degree, f32[1024,512]{1,0:T(8,128)} %copy-done, ...), custom_call_target="tpu_custom_call" | custom-call | tf_op jit(solution)/shard_map/apply/pallas_call | solution.py:186
  165.3 3.1 %collective-permute-start.24 = (f32[2,512]{1,0:T(2,128)S(1)}, f32[2,512]{1,0:T(2,128)S(1)}, u32[]{:S(2)}, u32[]{:S(2)}) collective-permute-start(f32[2,512]{1,0:T(2,128)S(1)} %pad_maximum_fusion.5), channel_id=1, source_target_pairs={{0,1},{1,0},{2,3},{3,2},{4,5},{5,4},{6,7},{7,6},{8,9},{9,8},{10,11... | collective-permute-start | bytes 12296 | tf_op jit(solution)/shard_map/ppermute | solution.py:17
  178.1 3.2 %collective-permute-done.29 = f32[2,512]{1,0:T(2,128)S(1)} collective-permute-done((f32[2,512]{1,0:T(2,128)S(1)}, f32[2,512]{1,0:T(2,128)S(1)}, u32[]{:S(2)}, u32[]{:S(2)}) %collective-permute-start.29) | collective-permute-done | bytes 4128 | tf_op jit(solution)/shard_map/ppermute | solution.py:17
  181.3 4.9 %collective-permute-start.33 = (f32[2,512]{1,0:T(2,128)S(1)}, f32[2,512]{1,0:T(2,128)S(1)}, u32[]{:S(2)}, u32[]{:S(2)}) collective-permute-start(f32[2,512]{1,0:T(2,128)S(1)} %add_add_fusion.3), channel_id=1, source_target_pairs={{0,192},{64,0},{128,64},{192,128},{1,193},{65,1},{129,65},{193,129... | collective-permute-start | bytes 12296 | tf_op jit(solution)/shard_map/ppermute | solution.py:17
  187.0 2.6 %collective-permute-done.32 = f32[2,512]{1,0:T(2,128)S(1)} collective-permute-done((f32[2,512]{1,0:T(2,128)S(1)}, f32[2,512]{1,0:T(2,128)S(1)}, u32[]{:S(2)}, u32[]{:S(2)}) %collective-permute-start.32) | collective-permute-done | bytes 4128 | tf_op jit(solution)/shard_map/ppermute | solution.py:17
  190.5 5.7 %collective-permute-start.34 = (f32[2,512]{1,0:T(2,128)S(1)}, f32[2,512]{1,0:T(2,128)S(1)}, u32[]{:S(2)}, u32[]{:S(2)}) collective-permute-start(f32[2,512]{1,0:T(2,128)S(1)} %add_add_fusion.2), channel_id=1, source_target_pairs={{0,2},{2,0},{1,3},{3,1},{4,6},{6,4},{5,7},{7,5},{8,10},{10,8},{9,1... | collective-permute-start | bytes 12296 | tf_op jit(solution)/shard_map/ppermute | solution.py:17
  198.8 2.4 %take_step.1 = (f32[1024,512]{1,0:T(8,128)}, f32[1024,512]{1,0:T(8,128)}) custom-call(f32[2,512]{1,0:T(2,128)S(1)} %add.286.sums, bf16[1024,512]{1,0:T(8,128)(2,1)S(1)} %bitcast.25, f32[1024,512]{1,0:T(8,128)S(1)} %copy-done.1, f32[1024,512]{1,0:T(8,128)S(1)} %copy-done.3), custom_call_target="tpu_custom_call" | custom-call | tf_op jit(solution)/shard_map/take_step/pallas_call | solution.py:223
  (102 shorter events, 56.2 us)
Async XLA Ops:
  6.4 5.6 %collective-permute-start = (f32[512,512]{1,0:T(8,128)S(1)}, f32[512,512]{1,0:T(8,128)S(1)}, u32[]{:S(2)}, u32[]{:S(2)}) collective-permute-start(f32[512,512]{1,0:T(8,128)S(1)} %constant_dynamic-slice_fusion.10), channel_id=1, source_target_pairs={{0,1},{1,0},{2,3},{3,2},{4,5},{5,4},{6,7},{7,6},{8,9},{9,8},{10,11... | collective-permute-start | bytes 3145736 | tf_op jit(solution)/shard_map/ppermute | solution.py:17
  13.5 9.5 %collective-permute-start.1 = (f32[128,512]{1,0:T(8,128)S(1)}, f32[128,512]{1,0:T(8,128)S(1)}, u32[]{:S(2)}, u32[]{:S(2)}) collective-permute-start(f32[128,512]{1,0:T(8,128)S(1)} %get-tuple-element.22), channel_id=1, source_target_pairs={{0,4},{4,8},{8,12},{12,0},{1,5},{5,9},{9,13},{13,1},{2,6},{6,10},{... | collective-permute-start | bytes 786440 | tf_op jit(solution)/shard_map/ppermute | solution.py:17
  13.6 9.5 %collective-permute-start.3 = (f32[128,512]{1,0:T(8,128)S(1)}, f32[128,512]{1,0:T(8,128)S(1)}, u32[]{:S(2)}, u32[]{:S(2)}) collective-permute-start(f32[128,512]{1,0:T(8,128)S(1)} %get-tuple-element.23), channel_id=1, source_target_pairs={{0,12},{4,0},{8,4},{12,8},{1,13},{5,1},{9,5},{13,9},{2,14},{6,2},{... | collective-permute-start | bytes 786440 | tf_op jit(solution)/shard_map/ppermute | solution.py:17
  16.3 11.1 %collective-permute-start.2 = (f32[128,512]{1,0:T(8,128)S(1)}, f32[128,512]{1,0:T(8,128)}, u32[]{:S(2)}, u32[]{:S(2)}) collective-permute-start(f32[128,512]{1,0:T(8,128)S(1)} %get-tuple-element.24), channel_id=1, source_target_pairs={{0,8},{4,12},{8,0},{12,4},{1,9},{5,13},{9,1},{13,5},{2,10},{6,14},... | collective-permute-start | bytes 786440 | tf_op jit(solution)/shard_map/ppermute | solution.py:17
  28.4 4.4 %collective-permute-start.4 = (f32[32,512]{1,0:T(8,128)S(1)}, f32[32,512]{1,0:T(8,128)S(1)}, u32[]{:S(2)}, u32[]{:S(2)}) collective-permute-start(f32[32,512]{1,0:T(8,128)S(1)} %get-tuple-element.25), channel_id=1, source_target_pairs={{0,16},{16,32},{32,48},{48,0},{1,17},{17,33},{33,49},{49,1},{2,18}... | collective-permute-start | bytes 196616 | tf_op jit(solution)/shard_map/ppermute | solution.py:17
  31.3 5.1 %collective-permute-start.5 = (f32[32,512]{1,0:T(8,128)S(1)}, f32[32,512]{1,0:T(8,128)S(1)}, u32[]{:S(2)}, u32[]{:S(2)}) collective-permute-start(f32[32,512]{1,0:T(8,128)S(1)} %get-tuple-element.27), channel_id=1, source_target_pairs={{0,32},{16,48},{32,0},{48,16},{1,33},{17,49},{33,1},{49,17},{2,34}... | collective-permute-start | bytes 196616 | tf_op jit(solution)/shard_map/ppermute | solution.py:17
  36.4 6.3 %collective-permute-start.7 = (f32[34,512]{1,0:T(8,128)S(1)}, f32[34,512]{1,0:T(8,128)S(1)}, u32[]{:S(2)}, u32[]{:S(2)}) collective-permute-start(f32[34,512]{1,0:T(8,128)S(1)} %get-tuple-element.28), channel_id=1, source_target_pairs={{0,64},{64,128},{128,192},{192,0},{1,65},{65,129},{129,193},{193,1... | collective-permute-start | bytes 208904 | tf_op jit(solution)/shard_map/ppermute | solution.py:17
  38.1 6.7 %collective-permute-start.8 = (f32[34,512]{1,0:T(8,128)S(1)}, f32[34,512]{1,0:T(8,128)S(1)}, u32[]{:S(2)}, u32[]{:S(2)}) collective-permute-start(f32[34,512]{1,0:T(8,128)S(1)} %get-tuple-element.29), channel_id=1, source_target_pairs={{0,128},{64,192},{128,0},{192,64},{1,129},{65,193},{129,1},{193,65... | collective-permute-start | bytes 208904 | tf_op jit(solution)/shard_map/ppermute | solution.py:17
  41.1 5.4 %collective-permute-start.9 = (f32[34,512]{1,0:T(8,128)S(1)}, f32[34,512]{1,0:T(8,128)S(1)}, u32[]{:S(2)}, u32[]{:S(2)}) collective-permute-start(f32[34,512]{1,0:T(8,128)S(1)} %get-tuple-element.30), channel_id=1, source_target_pairs={{0,192},{64,0},{128,64},{192,128},{1,193},{65,1},{129,65},{193,129... | collective-permute-start | bytes 208904 | tf_op jit(solution)/shard_map/ppermute | solution.py:17
  46.5 7.1 %collective-permute-start.10 = (f32[32,512]{1,0:T(8,128)S(1)}, f32[32,512]{1,0:T(8,128)S(1)}, u32[]{:S(2)}, u32[]{:S(2)}) collective-permute-start(f32[32,512]{1,0:T(8,128)S(1)} %slice.8), channel_id=1, source_target_pairs={{0,2},{2,0},{1,3},{3,1},{4,6},{6,4},{5,7},{7,5},{8,10},{10,8},{9,1... | collective-permute-start | bytes 196616 | tf_op jit(solution)/shard_map/ppermute | solution.py:17
  53.8 4.5 %collective-permute-start.12 = (bf16[32,512]{1,0:T(8,128)(2,1)S(1)}, bf16[32,512]{1,0:T(8,128)(2,1)S(1)}, u32[]{:S(2)}, u32[]{:S(2)}) collective-permute-start(bf16[32,512]{1,0:T(8,128)(2,1)S(1)} %get-tuple-element.21), channel_id=1, source_target_pairs={{0,32},{16,48},{32,0},{48,16},{1,33},{17,49},{33,1},{49,17},{2,34}... | collective-permute-start | bytes 98312 | tf_op jit(solution)/shard_map/ppermute | solution.py:17
  60.0 5.3 %collective-permute-start.15 = (bf16[128,512]{1,0:T(8,128)(2,1)S(1)}, bf16[128,512]{1,0:T(8,128)(2,1)S(1)}, u32[]{:S(2)}, u32[]{:S(2)}) collective-permute-start(bf16[128,512]{1,0:T(8,128)(2,1)S(1)} %constant_dynamic-update-slice_fusion), channel_id=1, source_target_pairs={{0,8},{4,12},{8,0},{12,4},{1,9},{5,13},{9,1},{13,5},{2,10},{6,14},... | collective-permute-start | bytes 393224 | tf_op jit(solution)/shard_map/ppermute | solution.py:17
  61.5 5.3 %collective-permute-start.14 = (bf16[128,512]{1,0:T(8,128)(2,1)S(1)}, bf16[128,512]{1,0:T(8,128)(2,1)S(1)}, u32[]{:S(2)}, u32[]{:S(2)}) collective-permute-start(bf16[128,512]{1,0:T(8,128)(2,1)S(1)} %constant_dynamic-update-slice_fusion), channel_id=1, source_target_pairs={{0,4},{4,8},{8,12},{12,0},{1,5},{5,9},{9,13},{13,1},{2,6},{6,10},{... | collective-permute-start | bytes 393224 | tf_op jit(solution)/shard_map/ppermute | solution.py:17
  66.8 9.1 %collective-permute-start.17 = (bf16[4,128,512]{2,1,0:T(8,128)(2,1)S(1)}, bf16[4,128,512]{2,1,0:T(8,128)(2,1)S(1)}, u32[]{:S(2)}, u32[]{:S(2)}) collective-permute-start(bf16[4,128,512]{2,1,0:T(8,128)(2,1)S(1)} %pad_maximum_fusion.mine), channel_id=1, source_target_pairs={{0,1},{1,0},{2,3},{3,2},{4,5},{5,4},{6,7},{7,6},{8,9},{9,8},{10,11... | collective-permute-start | bytes 1572872 | tf_op jit(solution)/shard_map/ppermute | solution.py:17
  81.4 26.4 %collective-permute-start.21 = (bf16[1024,512]{1,0:T(8,128)(2,1)S(1)}, bf16[1024,512]{1,0:T(8,128)(2,1)S(1)}, u32[]{:S(2)}, u32[]{:S(2)}) collective-permute-start(bf16[1024,512]{1,0:T(8,128)(2,1)S(1)} %get-tuple-element.15.own), channel_id=1, source_target_pairs={{64,0},{128,64},{192,128},{65,1},{129,65},{193,129},{66,2},{130,66... | collective-permute-start | bytes 3145736 | tf_op jit(solution)/shard_map/ppermute | solution.py:26
  82.8 26.3 %collective-permute-start.18 = (bf16[1024,512]{1,0:T(8,128)(2,1)S(1)}, bf16[1024,512]{1,0:T(8,128)(2,1)S(1)}, u32[]{:S(2)}, u32[]{:S(2)}) collective-permute-start(bf16[1024,512]{1,0:T(8,128)(2,1)S(1)} %get-tuple-element.15.own), channel_id=1, source_target_pairs={{0,64},{64,128},{128,192},{1,65},{65,129},{129,193},{2,66},{66,130... | collective-permute-start | bytes 3145736 | tf_op jit(solution)/shard_map/ppermute | solution.py:26
  107.8 25.4 %collective-permute-start.22 = (bf16[1024,512]{1,0:T(8,128)(2,1)S(1)}, bf16[1024,512]{1,0:T(8,128)(2,1)}, u32[]{:S(2)}, u32[]{:S(2)}) collective-permute-start(bf16[1024,512]{1,0:T(8,128)(2,1)S(1)} %collective-permute-done.21.r1), channel_id=1, source_target_pairs={{64,0},{128,64},{65,1},{129,65},{66,2},{130,66},{67,3},{131,67},{6... | collective-permute-start | bytes 3145736 | tf_op jit(solution)/shard_map/ppermute | solution.py:26
  109.1 25.4 %collective-permute-start.19 = (bf16[1024,512]{1,0:T(8,128)(2,1)S(1)}, bf16[1024,512]{1,0:T(8,128)(2,1)}, u32[]{:S(2)}, u32[]{:S(2)}) collective-permute-start(bf16[1024,512]{1,0:T(8,128)(2,1)S(1)} %collective-permute-done.18.l1), channel_id=1, source_target_pairs={{64,128},{128,192},{65,129},{129,193},{66,130},{130,194},{67,131},... | collective-permute-start | bytes 3145736 | tf_op jit(solution)/shard_map/ppermute | solution.py:26
  133.2 24.7 %collective-permute-start.23 = (bf16[1024,512]{1,0:T(8,128)(2,1)}, bf16[1024,512]{1,0:T(8,128)(2,1)}, u32[]{:S(2)}, u32[]{:S(2)}) collective-permute-start(bf16[1024,512]{1,0:T(8,128)(2,1)} %collective-permute-done.22.r2), channel_id=1, source_target_pairs={{64,0},{65,1},{66,2},{67,3},{68,4},{69,5},{70,6},{71,7},{72,8},{73... | collective-permute-start | bytes 3145736 | tf_op jit(solution)/shard_map/ppermute | solution.py:26
  134.5 23.4 %collective-permute-start.20 = (bf16[1024,512]{1,0:T(8,128)(2,1)}, bf16[1024,512]{1,0:T(8,128)(2,1)}, u32[]{:S(2)}, u32[]{:S(2)}) collective-permute-start(bf16[1024,512]{1,0:T(8,128)(2,1)} %collective-permute-done.19.l2), channel_id=1, source_target_pairs={{128,192},{129,193},{130,194},{131,195},{132,196},{133,197},{134,1... | collective-permute-start | bytes 3145736 | tf_op jit(solution)/shard_map/ppermute | solution.py:26
  169.3 4.0 %collective-permute-start.26 = (f32[2,512]{1,0:T(2,128)S(1)}, f32[2,512]{1,0:T(2,128)S(1)}, u32[]{:S(2)}, u32[]{:S(2)}) collective-permute-start(f32[2,512]{1,0:T(2,128)S(1)} %fusion.7), channel_id=1, source_target_pairs={{0,8},{4,12},{8,0},{12,4},{1,9},{5,13},{9,1},{13,5},{2,10},{6,14},... | collective-permute-start | bytes 12296 | tf_op jit(solution)/shard_map/ppermute | solution.py:17
  181.3 5.7 %collective-permute-start.33 = (f32[2,512]{1,0:T(2,128)S(1)}, f32[2,512]{1,0:T(2,128)S(1)}, u32[]{:S(2)}, u32[]{:S(2)}) collective-permute-start(f32[2,512]{1,0:T(2,128)S(1)} %add_add_fusion.3), channel_id=1, source_target_pairs={{0,192},{64,0},{128,64},{192,128},{1,193},{65,1},{129,65},{193,129... | collective-permute-start | bytes 12296 | tf_op jit(solution)/shard_map/ppermute | solution.py:17
  186.2 4.3 %collective-permute-start.31 = (f32[2,512]{1,0:T(2,128)S(1)}, f32[2,512]{1,0:T(2,128)S(1)}, u32[]{:S(2)}, u32[]{:S(2)}) collective-permute-start(f32[2,512]{1,0:T(2,128)S(1)} %add_add_fusion.3), channel_id=1, source_target_pairs={{0,64},{64,128},{128,192},{192,0},{1,65},{65,129},{129,193},{193,1... | collective-permute-start | bytes 12296 | tf_op jit(solution)/shard_map/ppermute | solution.py:17
  190.5 6.7 %collective-permute-start.34 = (f32[2,512]{1,0:T(2,128)S(1)}, f32[2,512]{1,0:T(2,128)S(1)}, u32[]{:S(2)}, u32[]{:S(2)}) collective-permute-start(f32[2,512]{1,0:T(2,128)S(1)} %add_add_fusion.2), channel_id=1, source_target_pairs={{0,2},{2,0},{1,3},{3,1},{4,6},{6,4},{5,7},{7,5},{8,10},{10,8},{9,1... | collective-permute-start | bytes 12296 | tf_op jit(solution)/shard_map/ppermute | solution.py:17
  (21 other events, 322.0 us)
